TPU v7x, 32 devices: a whole 2x2x4 slice. The times are simulated.
32 devices in a mesh: space: 8 (over z, x), member: 4 (over y, core).
Axes of the slice: x: 2, y: 2, z: 4, core: 2. Of those that a mesh axis runs over, the one named last changes fastest.
Arguments:
- fields: float32 [8, 16, 128, 256], P('member', 'space'), may hold values from -6 to 6
- velocity: float32 [16, 128, 256], P('space'), may hold values from 0.2 to 0.6
- building: int32 [16, 128, 256], P('space'), may hold values 0 or 1
- inflow_table: float32 [32, 128, 256], replicated, may hold values from -6 to 6
- inflow_index: int32 [8], P('member'), may hold values from 0 to 31
Outputs:
- fields_now: float32 [8, 16, 128, 256], P('member', 'space')
- r_factor: float32 [8, 8], replicated
All inputs are finite; a program needn't handle non-finite values. No bound on the sum of `building` on one device may be relied on, other than what follows from the above.
Results may differ from a plain program's by a relative error of at most 0.0003.
Values may be sent and summed in bfloat16 or wider, within the bound.
A program may use at most 64 MiB of HBM per device.

v0:
```python
import jax
import jax.numpy as jnp
from jax import lax
from jax.sharding import PartitionSpec as P

STEPS = 2
kappa_rate = 0.05
shrink_weight = 0.1
contract_dims = (((1,), (1,)), ((), ()))


def extended_2(block, sides, width):
    for axis, dim in sides:
        count = lax.axis_size(axis)
        forward = [(i, i + 1) for i in range(count - 1)]
        backward = [(target, source) for source, target in forward]
        low = lax.ppermute(
            lax.slice_in_dim(block, block.shape[dim] - width, None, axis=dim), axis, forward
        )
        high = lax.ppermute(lax.slice_in_dim(block, 0, width, axis=dim), axis, backward)
        block = jnp.concatenate([low, block, high], axis=dim)
    return block


def from_behind(block, axis, distance):
    devices = range(lax.axis_size(axis))
    route = [((i - distance) % len(devices), i) for i in devices]
    return lax.ppermute(block, axis, route)


def advance(extended, fluid_cells, courant):
    upwind = extended[:, :-2]
    centre = extended[:, 1:-1]
    downwind = extended[:, 2:]
    in_plane = (
        jnp.roll(centre, 1, 2)
        + jnp.roll(centre, -1, 2)
        + jnp.roll(centre, 1, 3)
        + jnp.roll(centre, -1, 3)
    )
    return fluid_cells * (
        centre
        + courant * (upwind - centre)
        + kappa_rate * (upwind + downwind + in_plane - 6.0 * centre)
    )


def local(fields, velocity, building, inflow_table, inflow_index):
    mem_dev = fields.shape[0]
    slab_depth = fields.shape[1]
    plane_rows = fields.shape[2]
    plane_cols = fields.shape[3]
    patterns = inflow_table.shape[0]
    fluid_cells = (1 - building).astype(jnp.float32)
    pattern_pick = (inflow_index[:, None] == jnp.arange(patterns, dtype=jnp.int32)[None, :]).astype(
        jnp.float32
    )
    inflow_plane = jnp.dot(
        pattern_pick,
        inflow_table.reshape(patterns, plane_rows * plane_cols),
        precision=lax.Precision.HIGHEST,
        preferred_element_type=jnp.float32,
    ).reshape(mem_dev, plane_rows, plane_cols)
    at_inflow = lax.axis_index("space") == 0
    fields_now = fields
    for sweep_index in range(STEPS):
        extended = extended_2(fields_now, (("space", 1),), 1)
        extended = extended.at[:, 0].set(jnp.where(at_inflow, inflow_plane, extended[:, 0]))
        fields_now = advance(extended, fluid_cells, velocity)
    groups = lax.axis_size("member")
    all_members = mem_dev * groups
    member_sum = jnp.sum(fields_now, 0)
    ensemble_mean = (
        lax.psum(member_sum.astype(jnp.bfloat16), "member").astype(jnp.float32) / all_members
    )
    anomaly = (
        (fields_now - ensemble_mean)
        .astype(jnp.bfloat16)
        .reshape(mem_dev, slab_depth * plane_rows * plane_cols)
    )
    my_group = lax.axis_index("member")
    cells_all = slab_depth * lax.axis_size("space") * plane_rows * plane_cols
    empty_rows = jnp.zeros((mem_dev, all_members), jnp.float32)

    def place(gram_tile, panel_piece, first_row):
        gram_block = lax.dot_general(
            anomaly, panel_piece, contract_dims, preferred_element_type=jnp.float32
        )
        return lax.dynamic_update_slice(
            gram_tile, gram_block, (jnp.int32(0), jnp.asarray(first_row))
        )

    gram_tile = place(empty_rows, anomaly, my_group * mem_dev)

    def turn(sweep_index, loop_state):
        tile_now, panel_held = loop_state
        panel_held = from_behind(panel_held, "member", 1)
        source = (my_group - sweep_index) % groups
        return (place(tile_now, panel_held, source * mem_dev), panel_held)

    gram_tile, panel_held = lax.fori_loop(1, groups, turn, (gram_tile, anomaly))
    gram_tile = gram_tile / cells_all
    summed = lax.psum(gram_tile, "space")
    gram_full = lax.all_gather(summed, "member", axis=0, tiled=True)
    r_factor = jnp.linalg.cholesky(
        gram_full + shrink_weight * jnp.eye(all_members, dtype=jnp.float32)
    ).T
    return (fields_now, r_factor)


def solution(mesh):
    placed = (
        P("member", "space", None, None),
        P("space", None, None),
        P("space", None, None),
        P(),
        P("member"),
    )
    return jax.shard_map(
        local,
        mesh=mesh,
        in_specs=placed,
        out_specs=(P("member", "space", None, None), P()),
        check_vma=False,
    )
```

profile of v0, /device:TPU:0, one launch (start us, length us, event | category | flops | bytes accessed | tf_op | source)
XLA Modules:
  0.0 151.2 jit_solution(6526579312249673913)
XLA Ops:
  7.2 1.4 copy.24
  8.9 4.9 %collective-permute-start.1 = (f32[2,1,128,256]{3,0,2,1:T(2,128)S(1)}, f32[2,1,128,256]{3,0,2,1:T(2,128)S(1)}, u32[]{:S(2)}, u32[]{:S(2)}) collective-permute-start(f32[2,1,128,256]{3,0,2,1:T(2,128)S(1)} %get-tuple-element.196), channel_id=1, source_target_pairs={{0,4},{4,8},{8,12},{12,16},{16,20},{20,24},{24,28},{1,5},{5,9},{9,... | collective-permute-start | bytes 786440 | tf_op jit(solution)/shard_map/ppermute | solution.py:17
  13.7 1.3 collective-permute-start.2
  15.0 1.0 subtract_convert_fusion.1
  16.0 8.9 %collective-permute-done.1 = f32[2,1,128,256]{3,0,2,1:T(2,128)S(1)} collective-permute-done((f32[2,1,128,256]{3,0,2,1:T(2,128)S(1)}, f32[2,1,128,256]{3,0,2,1:T(2,128)S(1)}, u32[]{:S(2)}, u32[]{:S(2)}) %collective-permute-start.1) | collective-permute-done | bytes 262176 | tf_op jit(solution)/shard_map/ppermute | solution.py:17
  25.4 6.0 %bitcast_dynamic-update-slice_fusion.1 = (f32[2,4,128,256]{3,0,2,1:T(2,128)S(1)}, f32[2,128,256]{2,0,1:T(2,128)S(1)}) fusion(f32[2,4,128,256]{3,0,2,1:T(2,128)S(1)} %pad_maximum_fusion, f32[2,1,128,256]{3,0,2,1:T(2,128)S(1)} %collective-permute-done.1, pred[]{:T(512)S(6)} %eq.25, s32[2]{0:T(128)S(1)} %copy-done.1, f32[4,8,128,256]{3,2,1,0:T(8,128)} %bitcast.51), kind=kOutput, calls=%fused_computation.27 | convolution fusion | flops 25231424 | bytes 4981249 | tf_op jit(solution)/shard_map/dot_general | solution.py:58
  32.7 1.9 %fusion.15 = f32[2,2,128,256]{3,0,2,1:T(2,128)S(1)} fusion(f32[2,2,128,1]{3,0,2,1:T(2,128)S(1)} %get-tuple-element.191, f32[2,2,128,255]{3,0,2,1:T(2,128)S(1)} %get-tuple-element.193, f32[2,2,128,255]{3,0,2,1:T(2,128)S(1)} %get-tuple-element.192, f32[2,2,128,1]{3,0,2,1:T(2,128)S(1)} %get-tuple-element.190, f32[2,2,1,256]{3,0,2,1:T(2,128)S(1)} %get-tuple-element.187, ...), kind=kLoop, calls=%fused_computation.23 | loop fusion | flops 2228224 | bytes 4718592 | tf_op jit(solution)/shard_map/mul | solution.py:41
  34.8 4.4 %collective-permute-start.3 = (f32[2,1,128,256]{3,0,2,1:T(2,128)S(1)}, f32[2,1,128,256]{3,0,2,1:T(2,128)S(1)}, u32[]{:S(2)}, u32[]{:S(2)}) collective-permute-start(f32[2,1,128,256]{3,0,2,1:T(2,128)S(1)} %get-tuple-element.194), channel_id=1, source_target_pairs={{0,4},{4,8},{8,12},{12,16},{16,20},{20,24},{24,28},{1,5},{5,9},{9,... | collective-permute-start | bytes 786440 | tf_op jit(solution)/shard_map/ppermute | solution.py:17
  39.3 1.5 collective-permute-start.4
  40.7 3.2 %collective-permute-done.3 = f32[2,1,128,256]{3,0,2,1:T(2,128)S(1)} collective-permute-done((f32[2,1,128,256]{3,0,2,1:T(2,128)S(1)}, f32[2,1,128,256]{3,0,2,1:T(2,128)S(1)}, u32[]{:S(2)}, u32[]{:S(2)}) %collective-permute-start.3) | collective-permute-done | bytes 262176 | tf_op jit(solution)/shard_map/ppermute | solution.py:17
  43.9 5.9 %collective-permute-done.4 = f32[2,1,128,256]{3,0,2,1:T(2,128)S(1)} collective-permute-done((f32[2,1,128,256]{3,0,2,1:T(2,128)S(1)}, f32[2,1,128,256]{3,0,2,1:T(2,128)S(1)}, u32[]{:S(2)}, u32[]{:S(2)}) %collective-permute-start.4) | collective-permute-done | bytes 262176 | tf_op jit(solution)/shard_map/ppermute | solution.py:20
  51.8 3.2 %fusion.22 = (bf16[2,128,256]{2,1,0:T(8,128)(2,1)}, f32[2,2,128,256]{3,0,2,1:T(2,128)S(1)}) fusion(f32[2,2,128,1]{3,0,2,1:T(2,128)S(1)} %get-tuple-element.183, f32[2,2,128,255]{3,0,2,1:T(2,128)S(1)} %get-tuple-element.185, f32[2,2,128,255]{3,0,2,1:T(2,128)S(1)} %get-tuple-element.184, f32[2,2,128,1]{3,0,2,1:T(2,128)S(1)} %get-tuple-element.182, ...), kind=kLoop, calls=%fused_computation.44 | loop fusion | flops 2293760 | bytes 4849664 | tf_op jit(solution)/shard_map/reduce_sum | solution.py:72
  55.0 35.5 %all-reduce.2.cloned.1.call-done = bf16[2,128,256]{2,1,0:T(8,128)(2,1)} async-done(((bf16[2,128,256]{2,1,0:T(8,128)(2,1)}), bf16[2,128,256]{2,1,0:T(8,128)(2,1)}) %all-reduce.2.cloned.1.call-update) | async-done | bytes 131088 | tf_op jit(solution)/shard_map/psum | solution.py:74
  90.5 0.9 convert_multiply_fusion
  91.7 0.9 convolution_bitcast_fusion
  92.9 21.1 %while.19 = (s32[]{:T(128)}, f32[2,8]{1,0:T(2,128)S(1)}, bf16[2,65536]{1,0:T(2,128)(2,1)S(1)}, bf16[2,65536]{1,0:T(2,128)(2,1)S(1)}, s32[]{:T(128)}, /*index=5*/...) while((s32[]{:T(128)}, f32[2,8]{1,0:T(2,128)S(1)}, ...), condition=%wide.region_3.4_spmd, body=%wide.region_2.3_spmd.sunk | while | flops 524306 | bytes 2097520 | solution.py:101
  93.0 5.8 %collective-permute-done = bf16[2,65536]{1,0:T(2,128)(2,1)S(1)} collective-permute-done((bf16[2,65536]{1,0:T(2,128)(2,1)S(1)}, bf16[2,65536]{1,0:T(2,128)(2,1)S(1)}, u32[]{:S(2)}, u32[]{:S(2)}) %collective-permute-start) | collective-permute-done | bytes 262176 | tf_op jit(solution)/shard_map/while/body/eval_jaxpr/ppermute | solution.py:28
  98.8 0.8 fusion.44
  100.0 5.8 %collective-permute-done = bf16[2,65536]{1,0:T(2,128)(2,1)S(1)} collective-permute-done((bf16[2,65536]{1,0:T(2,128)(2,1)S(1)}, bf16[2,65536]{1,0:T(2,128)(2,1)S(1)}, u32[]{:S(2)}, u32[]{:S(2)}) %collective-permute-start) | collective-permute-done | bytes 262176 | tf_op jit(solution)/shard_map/while/body/eval_jaxpr/ppermute | solution.py:28
  107.1 5.8 %collective-permute-done = bf16[2,65536]{1,0:T(2,128)(2,1)S(1)} collective-permute-done((bf16[2,65536]{1,0:T(2,128)(2,1)S(1)}, bf16[2,65536]{1,0:T(2,128)(2,1)S(1)}, u32[]{:S(2)}, u32[]{:S(2)}) %collective-permute-start) | collective-permute-done | bytes 262176 | tf_op jit(solution)/shard_map/while/body/eval_jaxpr/ppermute | solution.py:28
  114.0 0.8 copy.32
  114.9 21.3 %psum.15 = f32[2,8]{1,0:T(2,128)S(1)} all-reduce(f32[2,8]{1,0:T(2,128)S(1)} %broadcast_multiply_fusion), channel_id=1, replica_groups=mesh['space'=8,'member'=4] {'space'}, use_global_device_ids=true, to_apply=%region_4.5 | all-reduce | flops 16 | bytes 128 | tf_op jit(solution)/shard_map/psum | solution.py:103
  136.2 5.1 %all-gather = f32[4,2,8]{2,1,0:T(2,128)S(1)} all-gather(f32[1,2,8]{2,1,0:T(2,128)S(1)} %bitcast.55), channel_id=1, replica_groups=mesh['space'=8,'member'=4] {'member'}, dimensions={0}, use_global_device_ids=true | all-gather | bytes 320 | tf_op jit(solution)/shard_map/all_gather | solution.py:104
  143.1 1.3 select_bitcast_fusion
  (44 shorter events, 9.5 us)
Async XLA Ops:
  7.2 18.2 %copy-start.1 = (s32[2]{0:T(128)S(1)}, s32[2]{0:T(128)}, u32[]{:S(2)}) copy-start(s32[2]{0:T(128)} %param.15) | copy-start | bytes 28
  7.2 83.3 %all-reduce.2.cloned.1.call-start = ((), (), s32[]{:S(2)}) async-start(), calls=%async_computation | async-start | bytes 262144 | tf_op jit(solution)/shard_map/psum | solution.py:74
  8.9 16.0 %collective-permute-start.1 = (f32[2,1,128,256]{3,0,2,1:T(2,128)S(1)}, f32[2,1,128,256]{3,0,2,1:T(2,128)S(1)}, u32[]{:S(2)}, u32[]{:S(2)}) collective-permute-start(f32[2,1,128,256]{3,0,2,1:T(2,128)S(1)} %get-tuple-element.196), channel_id=1, source_target_pairs={{0,4},{4,8},{8,12},{12,16},{16,20},{20,24},{24,28},{1,5},{5,9},{9,... | collective-permute-start | bytes 786440 | tf_op jit(solution)/shard_map/ppermute | solution.py:17
  13.7 11.2 %collective-permute-start.2 = (f32[2,1,128,256]{3,0,2,1:T(2,128)S(1)}, f32[2,1,128,256]{3,0,2,1:T(2,128)S(1)}, u32[]{:S(2)}, u32[]{:S(2)}) collective-permute-start(f32[2,1,128,256]{3,0,2,1:T(2,128)S(1)} %get-tuple-element.197), channel_id=1, source_target_pairs={{4,0},{8,4},{12,8},{16,12},{20,16},{24,20},{28,24},{5,1},{9,5},{13... | collective-permute-start | bytes 786440 | tf_op jit(solution)/shard_map/ppermute | solution.py:20
  25.4 7.3 %copy-start = (f32[2,128,256]{2,1,0:T(8,128)S(1)}, f32[2,128,256]{2,1,0:T(8,128)}, u32[]{:S(2)}) copy-start(f32[2,128,256]{2,1,0:T(8,128)} %param.12) | copy-start | bytes 786436
  34.8 9.1 %collective-permute-start.3 = (f32[2,1,128,256]{3,0,2,1:T(2,128)S(1)}, f32[2,1,128,256]{3,0,2,1:T(2,128)S(1)}, u32[]{:S(2)}, u32[]{:S(2)}) collective-permute-start(f32[2,1,128,256]{3,0,2,1:T(2,128)S(1)} %get-tuple-element.194), channel_id=1, source_target_pairs={{0,4},{4,8},{8,12},{12,16},{16,20},{20,24},{24,28},{1,5},{5,9},{9,... | collective-permute-start | bytes 786440 | tf_op jit(solution)/shard_map/ppermute | solution.py:17
  39.3 10.5 %collective-permute-start.4 = (f32[2,1,128,256]{3,0,2,1:T(2,128)S(1)}, f32[2,1,128,256]{3,0,2,1:T(2,128)S(1)}, u32[]{:S(2)}, u32[]{:S(2)}) collective-permute-start(f32[2,1,128,256]{3,0,2,1:T(2,128)S(1)} %get-tuple-element.195), channel_id=1, source_target_pairs={{4,0},{8,4},{12,8},{16,12},{20,16},{24,20},{28,24},{5,1},{9,5},{13... | collective-permute-start | bytes 786440 | tf_op jit(solution)/shard_map/ppermute | solution.py:20
  92.9 5.8 %collective-permute-start = (bf16[2,65536]{1,0:T(2,128)(2,1)S(1)}, bf16[2,65536]{1,0:T(2,128)(2,1)S(1)}, u32[]{:S(2)}, u32[]{:S(2)}) collective-permute-start(bf16[2,65536]{1,0:T(2,128)(2,1)S(1)} %get-tuple-element.244), channel_id=1, source_target_pairs={{3,0},{0,1},{1,2},{2,3},{7,4},{4,5},{5,6},{6,7},{11,8},{8,9},{9,10... | collective-permute-start | bytes 786440 | tf_op jit(solution)/shard_map/while/body/eval_jaxpr/ppermute | solution.py:28
  99.9 5.8 %collective-permute-start = (bf16[2,65536]{1,0:T(2,128)(2,1)S(1)}, bf16[2,65536]{1,0:T(2,128)(2,1)S(1)}, u32[]{:S(2)}, u32[]{:S(2)}) collective-permute-start(bf16[2,65536]{1,0:T(2,128)(2,1)S(1)} %get-tuple-element.244), channel_id=1, source_target_pairs={{3,0},{0,1},{1,2},{2,3},{7,4},{4,5},{5,6},{6,7},{11,8},{8,9},{9,10... | collective-permute-start | bytes 786440 | tf_op jit(solution)/shard_map/while/body/eval_jaxpr/ppermute | solution.py:28
  107.0 5.8 %collective-permute-start = (bf16[2,65536]{1,0:T(2,128)(2,1)S(1)}, bf16[2,65536]{1,0:T(2,128)(2,1)S(1)}, u32[]{:S(2)}, u32[]{:S(2)}) collective-permute-start(bf16[2,65536]{1,0:T(2,128)(2,1)S(1)} %get-tuple-element.244), channel_id=1, source_target_pairs={{3,0},{0,1},{1,2},{2,3},{7,4},{4,5},{5,6},{6,7},{11,8},{8,9},{9,10... | collective-permute-start | bytes 786440 | tf_op jit(solution)/shard_map/while/body/eval_jaxpr/ppermute | solution.py:28
Sparse Core Ops, SparseCore 0:
  55.1 35.3 all-reduce.1
where the time goes:
time: 151 us
  waiting for transfers between devices  70.7 us (47%)
  blocking collectives  26.4 us (17%)
  between operations  14.3 us (9%)
  starting transfers between devices  12.2 us (8%)
  other arithmetic  11.2 us (7%)
  matrix products  9.16 us (6%)
  local copies, waits for them, and re-layouts  7.04 us (5%)
    psum x1, waiting for transfers between devices, local(): lax.psum(member_sum.astype(jnp.bfloat16), 'member').astype(jnp.float32)  35.5 us
    psum x1, blocking collectives, local(): summed = lax.psum(gram_tile, 'space')  21.3 us
    ppermute x3, waiting for transfers between devices, from_behind(): return lax.ppermute(block, axis, route)  17.3 us
    ppermute x2, waiting for transfers between devices, extended_2(): lax.ppermute(lax.slice_in_dim(block, block.shape[dim] - width, None, axis...  12 us
    ppermute x2, starting transfers between devices, extended_2(): lax.ppermute(lax.slice_in_dim(block, block.shape[dim] - width, None, axis...  9.26 us
    dot_general x1, matrix products, local(): jnp.dot(pattern_pick, inflow_table.reshape(patterns, plane_rows * plane_c...  5.97 us
    ppermute x2, waiting for transfers between devices, extended_2(): lax.ppermute(lax.slice_in_dim(block, 0, width, axis=dim), axis, backward)  5.88 us
    all_gather x1, blocking collectives, local(): gram_full = lax.all_gather(summed, 'member', axis=0, tiled=True)  5.06 us
  transfers between devices with their start and end apart: 8, of which 7 were waited for; matrix products, arithmetic and copies ran while one was open for 1% of the time, Pallas kernels for 0%

commit v1 on v0

--- a/solution.py
+++ b/solution.py
@@ -1,12 +1,22 @@
+import functools
 import jax
 import jax.numpy as jnp
 from jax import lax
 from jax.sharding import PartitionSpec as P
+from jax.lax import all_gather
 
 STEPS = 2
 kappa_rate = 0.05
 shrink_weight = 0.1
 contract_dims = (((1,), (1,)), ((), ()))
+
+
+def number_slots_for(z_in, named_axis):
+    state_now = all_gather(z_in, axis_name=named_axis)
+    return jnp.sum(state_now, axis=0)
+
+
+lift_teams_over_axis = functools.partial(number_slots_for, named_axis="member")
 
 
 def extended_2(block, sides, width):
@@ -71,7 +81,7 @@
     all_members = mem_dev * groups
     member_sum = jnp.sum(fields_now, 0)
     ensemble_mean = (
-        lax.psum(member_sum.astype(jnp.bfloat16), "member").astype(jnp.float32) / all_members
+        lift_teams_over_axis(member_sum.astype(jnp.bfloat16)).astype(jnp.float32) / all_members
     )
     anomaly = (
         (fields_now - ensemble_mean)

time: 151 us -> 110 us (0.73)
  waiting for transfers between devices: 70.7 us -> 35 us
  between operations: 14.3 us -> 0.89 us
  blocking collectives: 26.4 us -> 35.7 us
  other arithmetic: 11.2 us -> 9.55 us
    psum x1 -> x0, waiting for transfers between devices: 35.5 us -> none  [local(): lax.psum(member_sum.astype(jnp.bfloat16), 'member').astype(jnp.float32)]
    all_gather x0 -> x1, blocking collectives: none -> 7.38 us  [number_slots_for(): state_now = all_gather(z_in, axis_name=named_axis)]
    psum x1, blocking collectives: 21.3 us -> 23.3 us  [local(): summed = lax.psum(gram_tile, 'space')]
  transfers between devices with their start and end apart: 8 -> 7, of which waited for: 7 -> 6; matrix products, arithmetic and copies ran while one was open for 1% -> 1% of each run, Pallas kernels for 0% -> 0%
where the time goes in v1:
time: 110 us
  blocking collectives  35.7 us (32%)
  waiting for transfers between devices  35 us (32%)
  starting transfers between devices  12.4 us (11%)
  other arithmetic  9.55 us (9%)
  matrix products  9.16 us (8%)
  local copies, waits for them, and re-layouts  7.05 us (6%)
    psum x1, blocking collectives, local(): summed = lax.psum(gram_tile, 'space')  23.3 us
    ppermute x3, waiting for transfers between devices, from_behind(): return lax.ppermute(block, axis, route)  16.9 us
    ppermute x2, waiting for transfers between devices, extended_2(): lax.ppermute(lax.slice_in_dim(block, block.shape[dim] - width, None, axis...  12.2 us
    ppermute x2, starting transfers between devices, extended_2(): lax.ppermute(lax.slice_in_dim(block, block.shape[dim] - width, None, axis...  9.26 us
    all_gather x1, blocking collectives, number_slots_for(): state_now = all_gather(z_in, axis_name=named_axis)  7.38 us
    dot_general x1, matrix products, local(): jnp.dot(pattern_pick, inflow_table.reshape(patterns, plane_rows * plane_c...  5.97 us
    ppermute x2, waiting for transfers between devices, extended_2(): lax.ppermute(lax.slice_in_dim(block, 0, width, axis=dim), axis, backward)  5.88 us
    all_gather x1, blocking collectives, local(): gram_full = lax.all_gather(summed, 'member', axis=0, tiled=True)  5.06 us
  transfers between devices with their start and end apart: 7, of which 6 were waited for; matrix products, arithmetic and copies ran while one was open for 1% of the time, Pallas kernels for 0%

profile of v1, /device:TPU:0, one launch (start us, length us, event | category | flops | bytes accessed | tf_op | source)
XLA Modules:
  0.0 109.9 jit_solution(15903435040732537734)
XLA Ops:
  0.6 1.5 %copy.24 = f32[2,2,128,256]{3,0,2,1:T(2,128)S(1)} copy(f32[2,2,128,256]{3,2,1,0:T(8,128)} %param.11) | data formatting | bytes 1048576 | tf_op args[0]
  2.3 4.9 %collective-permute-start.1 = (f32[2,1,128,256]{3,0,2,1:T(2,128)S(1)}, f32[2,1,128,256]{3,0,2,1:T(2,128)S(1)}, u32[]{:S(2)}, u32[]{:S(2)}) collective-permute-start(f32[2,1,128,256]{3,0,2,1:T(2,128)S(1)} %get-tuple-element.196), channel_id=1, source_target_pairs={{0,4},{4,8},{8,12},{12,16},{16,20},{20,24},{24,28},{1,5},{5,9},{9,... | collective-permute-start | bytes 786440 | tf_op jit(solution)/shard_map/ppermute | solution.py:27
  7.2 1.3 %collective-permute-start.2 = (f32[2,1,128,256]{3,0,2,1:T(2,128)S(1)}, f32[2,1,128,256]{3,0,2,1:T(2,128)S(1)}, u32[]{:S(2)}, u32[]{:S(2)}) collective-permute-start(f32[2,1,128,256]{3,0,2,1:T(2,128)S(1)} %get-tuple-element.197), channel_id=1, source_target_pairs={{4,0},{8,4},{12,8},{16,12},{20,16},{24,20},{28,24},{5,1},{9,5},{13... | collective-permute-start | bytes 786440 | tf_op jit(solution)/shard_map/ppermute | solution.py:30
  8.5 1.0 subtract_convert_fusion.1
  9.4 8.9 %collective-permute-done.1 = f32[2,1,128,256]{3,0,2,1:T(2,128)S(1)} collective-permute-done((f32[2,1,128,256]{3,0,2,1:T(2,128)S(1)}, f32[2,1,128,256]{3,0,2,1:T(2,128)S(1)}, u32[]{:S(2)}, u32[]{:S(2)}) %collective-permute-start.1) | collective-permute-done | bytes 262176 | tf_op jit(solution)/shard_map/ppermute | solution.py:27
  18.8 6.0 %bitcast_dynamic-update-slice_fusion.1 = (f32[2,4,128,256]{3,0,2,1:T(2,128)S(1)}, f32[2,128,256]{2,0,1:T(2,128)S(1)}) fusion(f32[2,4,128,256]{3,0,2,1:T(2,128)S(1)} %pad_maximum_fusion, f32[2,1,128,256]{3,0,2,1:T(2,128)S(1)} %collective-permute-done.1, pred[]{:T(512)S(6)} %eq.25, s32[2]{0:T(128)S(1)} %copy-done.1, f32[4,8,128,256]{3,2,1,0:T(8,128)} %bitcast.52), kind=kOutput, calls=%fused_computation.27 | convolution fusion | flops 25231424 | bytes 4981249 | tf_op jit(solution)/shard_map/dot_general | solution.py:68
  26.1 1.9 %fusion.15 = f32[2,2,128,256]{3,0,2,1:T(2,128)S(1)} fusion(f32[2,2,128,1]{3,0,2,1:T(2,128)S(1)} %get-tuple-element.191, f32[2,2,128,255]{3,0,2,1:T(2,128)S(1)} %get-tuple-element.193, f32[2,2,128,255]{3,0,2,1:T(2,128)S(1)} %get-tuple-element.192, f32[2,2,128,1]{3,0,2,1:T(2,128)S(1)} %get-tuple-element.190, f32[2,2,1,256]{3,0,2,1:T(2,128)S(1)} %get-tuple-element.187, ...), kind=kLoop, calls=%fused_computation.23 | loop fusion | flops 2228224 | bytes 4718592 | tf_op jit(solution)/shard_map/mul | solution.py:51
  28.3 4.4 %collective-permute-start.3 = (f32[2,1,128,256]{3,0,2,1:T(2,128)S(1)}, f32[2,1,128,256]{3,0,2,1:T(2,128)S(1)}, u32[]{:S(2)}, u32[]{:S(2)}) collective-permute-start(f32[2,1,128,256]{3,0,2,1:T(2,128)S(1)} %get-tuple-element.194), channel_id=1, source_target_pairs={{0,4},{4,8},{8,12},{12,16},{16,20},{20,24},{24,28},{1,5},{5,9},{9,... | collective-permute-start | bytes 786440 | tf_op jit(solution)/shard_map/ppermute | solution.py:27
  32.7 1.3 %collective-permute-start.4 = (f32[2,1,128,256]{3,0,2,1:T(2,128)S(1)}, f32[2,1,128,256]{3,0,2,1:T(2,128)S(1)}, u32[]{:S(2)}, u32[]{:S(2)}) collective-permute-start(f32[2,1,128,256]{3,0,2,1:T(2,128)S(1)} %get-tuple-element.195), channel_id=1, source_target_pairs={{4,0},{8,4},{12,8},{16,12},{20,16},{24,20},{28,24},{5,1},{9,5},{13... | collective-permute-start | bytes 786440 | tf_op jit(solution)/shard_map/ppermute | solution.py:30
  34.0 3.4 %collective-permute-done.3 = f32[2,1,128,256]{3,0,2,1:T(2,128)S(1)} collective-permute-done((f32[2,1,128,256]{3,0,2,1:T(2,128)S(1)}, f32[2,1,128,256]{3,0,2,1:T(2,128)S(1)}, u32[]{:S(2)}, u32[]{:S(2)}) %collective-permute-start.3) | collective-permute-done | bytes 262176 | tf_op jit(solution)/shard_map/ppermute | solution.py:27
  37.3 5.9 %collective-permute-done.4 = f32[2,1,128,256]{3,0,2,1:T(2,128)S(1)} collective-permute-done((f32[2,1,128,256]{3,0,2,1:T(2,128)S(1)}, f32[2,1,128,256]{3,0,2,1:T(2,128)S(1)}, u32[]{:S(2)}, u32[]{:S(2)}) %collective-permute-start.4) | collective-permute-done | bytes 262176 | tf_op jit(solution)/shard_map/ppermute | solution.py:30
  45.2 2.5 %fusion.22 = (bf16[2,128,256]{2,1,0:T(8,128)(2,1)S(1)}, f32[2,2,128,256]{3,0,2,1:T(2,128)S(1)}) fusion(f32[2,2,128,1]{3,0,2,1:T(2,128)S(1)} %get-tuple-element.183, f32[2,2,128,255]{3,0,2,1:T(2,128)S(1)} %get-tuple-element.185, f32[2,2,128,255]{3,0,2,1:T(2,128)S(1)} %get-tuple-element.184, f32[2,2,128,1]{3,0,2,1:T(2,128)S(1)} %get-tuple-element.182, ...), kind=kLoop, calls=%fused_computation.44 | loop fusion | flops 2293760 | bytes 4849664 | tf_op jit(solution)/shard_map/reduce_sum | solution.py:82
  47.7 7.4 %all-gather = bf16[8,128,256]{2,1,0:T(8,128)(2,1)S(1)} all-gather(bf16[2,128,256]{2,1,0:T(8,128)(2,1)S(1)} %get-tuple-element.176), channel_id=2, replica_groups=mesh['space'=8,'member'=4] {'member'}, dimensions={0}, use_global_device_ids=true | all-gather | bytes 655360 | tf_op jit(solution)/shard_map/all_gather | solution.py:15
  55.5 0.9 convolution_bitcast_fusion
  56.7 21.1 %while.19 = (s32[]{:T(128)}, f32[2,8]{1,0:T(2,128)S(1)}, bf16[2,65536]{1,0:T(2,128)(2,1)S(1)}, bf16[2,65536]{1,0:T(2,128)(2,1)S(1)}, s32[]{:T(128)}, /*index=5*/...) while((s32[]{:T(128)}, f32[2,8]{1,0:T(2,128)S(1)}, ...), condition=%wide.region_3.4_spmd, body=%wide.region_2.3_spmd.sunk | while | flops 524306 | bytes 2097520 | solution.py:111
  57.2 5.4 %collective-permute-done = bf16[2,65536]{1,0:T(2,128)(2,1)S(1)} collective-permute-done((bf16[2,65536]{1,0:T(2,128)(2,1)S(1)}, bf16[2,65536]{1,0:T(2,128)(2,1)S(1)}, u32[]{:S(2)}, u32[]{:S(2)}) %collective-permute-start) | collective-permute-done | bytes 262176 | tf_op jit(solution)/shard_map/while/body/eval_jaxpr/ppermute | solution.py:38
  63.9 5.8 %collective-permute-done = bf16[2,65536]{1,0:T(2,128)(2,1)S(1)} collective-permute-done((bf16[2,65536]{1,0:T(2,128)(2,1)S(1)}, bf16[2,65536]{1,0:T(2,128)(2,1)S(1)}, u32[]{:S(2)}, u32[]{:S(2)}) %collective-permute-start) | collective-permute-done | bytes 262176 | tf_op jit(solution)/shard_map/while/body/eval_jaxpr/ppermute | solution.py:38
  69.6 0.8 fusion.44
  70.9 5.8 %collective-permute-done = bf16[2,65536]{1,0:T(2,128)(2,1)S(1)} collective-permute-done((bf16[2,65536]{1,0:T(2,128)(2,1)S(1)}, bf16[2,65536]{1,0:T(2,128)(2,1)S(1)}, u32[]{:S(2)}, u32[]{:S(2)}) %collective-permute-start) | collective-permute-done | bytes 262176 | tf_op jit(solution)/shard_map/while/body/eval_jaxpr/ppermute | solution.py:38
  76.7 0.8 fusion.44
  77.9 0.8 copy.32
  78.7 23.3 %psum.7 = f32[2,8]{1,0:T(2,128)S(1)} all-reduce(f32[2,8]{1,0:T(2,128)S(1)} %broadcast_multiply_fusion), channel_id=1, replica_groups=mesh['space'=8,'member'=4] {'space'}, use_global_device_ids=true, to_apply=%region_4.5 | all-reduce | flops 16 | bytes 128 | tf_op jit(solution)/shard_map/psum | solution.py:113
  102.0 5.1 %all-gather.1 = f32[4,2,8]{2,1,0:T(2,128)S(1)} all-gather(f32[1,2,8]{2,1,0:T(2,128)S(1)} %bitcast.57), channel_id=1, replica_groups=mesh['space'=8,'member'=4] {'member'}, dimensions={0}, use_global_device_ids=true | all-gather | bytes 320 | tf_op jit(solution)/shard_map/all_gather | solution.py:114
  108.7 1.2 %select_bitcast_fusion = f32[8,8]{1,0:T(8,128)} fusion(f32[8,8]{0,1:T(8,128)S(1)} %copy.30, pred[]{:T(512)} %compare_reduce_fusion), kind=kLoop, calls=%fused_computation.33 | loop fusion | flops 192 | bytes 513 | tf_op jit(solution)/shard_map/transpose | solution.py:117
  (43 shorter events, 9.1 us)
Async XLA Ops:
  0.6 18.2 %copy-start.1 = (s32[2]{0:T(128)S(1)}, s32[2]{0:T(128)}, u32[]{:S(2)}) copy-start(s32[2]{0:T(128)} %param.15) | copy-start | bytes 28
  2.3 16.0 %collective-permute-start.1 = (f32[2,1,128,256]{3,0,2,1:T(2,128)S(1)}, f32[2,1,128,256]{3,0,2,1:T(2,128)S(1)}, u32[]{:S(2)}, u32[]{:S(2)}) collective-permute-start(f32[2,1,128,256]{3,0,2,1:T(2,128)S(1)} %get-tuple-element.196), channel_id=1, source_target_pairs={{0,4},{4,8},{8,12},{12,16},{16,20},{20,24},{24,28},{1,5},{5,9},{9,... | collective-permute-start | bytes 786440 | tf_op jit(solution)/shard_map/ppermute | solution.py:27
  7.2 11.2 %collective-permute-start.2 = (f32[2,1,128,256]{3,0,2,1:T(2,128)S(1)}, f32[2,1,128,256]{3,0,2,1:T(2,128)S(1)}, u32[]{:S(2)}, u32[]{:S(2)}) collective-permute-start(f32[2,1,128,256]{3,0,2,1:T(2,128)S(1)} %get-tuple-element.197), channel_id=1, source_target_pairs={{4,0},{8,4},{12,8},{16,12},{20,16},{24,20},{28,24},{5,1},{9,5},{13... | collective-permute-start | bytes 786440 | tf_op jit(solution)/shard_map/ppermute | solution.py:30
  18.8 7.3 %copy-start = (f32[2,128,256]{2,1,0:T(8,128)S(1)}, f32[2,128,256]{2,1,0:T(8,128)}, u32[]{:S(2)}) copy-start(f32[2,128,256]{2,1,0:T(8,128)} %param.12) | copy-start | bytes 786436
  28.3 9.1 %collective-permute-start.3 = (f32[2,1,128,256]{3,0,2,1:T(2,128)S(1)}, f32[2,1,128,256]{3,0,2,1:T(2,128)S(1)}, u32[]{:S(2)}, u32[]{:S(2)}) collective-permute-start(f32[2,1,128,256]{3,0,2,1:T(2,128)S(1)} %get-tuple-element.194), channel_id=1, source_target_pairs={{0,4},{4,8},{8,12},{12,16},{16,20},{20,24},{24,28},{1,5},{5,9},{9,... | collective-permute-start | bytes 786440 | tf_op jit(solution)/shard_map/ppermute | solution.py:27
  32.7 10.5 %collective-permute-start.4 = (f32[2,1,128,256]{3,0,2,1:T(2,128)S(1)}, f32[2,1,128,256]{3,0,2,1:T(2,128)S(1)}, u32[]{:S(2)}, u32[]{:S(2)}) collective-permute-start(f32[2,1,128,256]{3,0,2,1:T(2,128)S(1)} %get-tuple-element.195), channel_id=1, source_target_pairs={{4,0},{8,4},{12,8},{16,12},{20,16},{24,20},{28,24},{5,1},{9,5},{13... | collective-permute-start | bytes 786440 | tf_op jit(solution)/shard_map/ppermute | solution.py:30
  56.8 5.8 %collective-permute-start = (bf16[2,65536]{1,0:T(2,128)(2,1)S(1)}, bf16[2,65536]{1,0:T(2,128)(2,1)S(1)}, u32[]{:S(2)}, u32[]{:S(2)}) collective-permute-start(bf16[2,65536]{1,0:T(2,128)(2,1)S(1)} %get-tuple-element.244), channel_id=1, source_target_pairs={{3,0},{0,1},{1,2},{2,3},{7,4},{4,5},{5,6},{6,7},{11,8},{8,9},{9,10... | collective-permute-start | bytes 786440 | tf_op jit(solution)/shard_map/while/body/eval_jaxpr/ppermute | solution.py:38
  63.8 5.8 %collective-permute-start = (bf16[2,65536]{1,0:T(2,128)(2,1)S(1)}, bf16[2,65536]{1,0:T(2,128)(2,1)S(1)}, u32[]{:S(2)}, u32[]{:S(2)}) collective-permute-start(bf16[2,65536]{1,0:T(2,128)(2,1)S(1)} %get-tuple-element.244), channel_id=1, source_target_pairs={{3,0},{0,1},{1,2},{2,3},{7,4},{4,5},{5,6},{6,7},{11,8},{8,9},{9,10... | collective-permute-start | bytes 786440 | tf_op jit(solution)/shard_map/while/body/eval_jaxpr/ppermute | solution.py:38
  70.8 5.8 %collective-permute-start = (bf16[2,65536]{1,0:T(2,128)(2,1)S(1)}, bf16[2,65536]{1,0:T(2,128)(2,1)S(1)}, u32[]{:S(2)}, u32[]{:S(2)}) collective-permute-start(bf16[2,65536]{1,0:T(2,128)(2,1)S(1)} %get-tuple-element.244), channel_id=1, source_target_pairs={{3,0},{0,1},{1,2},{2,3},{7,4},{4,5},{5,6},{6,7},{11,8},{8,9},{9,10... | collective-permute-start | bytes 786440 | tf_op jit(solution)/shard_map/while/body/eval_jaxpr/ppermute | solution.py:38
